TPU v7x, 32 devices: a whole 2x2x4 slice. The times are simulated.
32 devices in a mesh: space: 4 (over z), batch: 8 (over y, x, core).
Axes of the slice: x: 2, y: 2, z: 4, core: 2. Of those that a mesh axis runs over, the one named last changes fastest.
Arguments:
- volume: bfloat16 [8, 4, 32, 32, 128], P('batch', None, 'space'), may hold values from -6 to 6
- kernel: bfloat16 [32, 108], replicated, may hold values from -0.625 to 0.625
- bias: float32 [32], replicated, may hold values from -3 to 3
- cotangent: bfloat16 [8, 32, 16, 1024], P('batch', 'space'), may hold values from -0.3515625 to 0.3515625
Outputs:
- pooled: bfloat16 [8, 32, 16, 1024], P('batch', 'space')
- kernel_grad: float32 [32, 108], replicated
- bias_grad: float32 [32], replicated
All inputs are finite; a program needn't handle non-finite values.
Results may differ from a plain program's by a relative error of at most 0.0065.
Values may be sent and summed in bfloat16 or wider, within the bound.
A program may use at most 64 MiB of HBM per device.

v0:
```python
import jax
import jax.numpy as jnp
from jax import lax
from jax.sharding import PartitionSpec as P

TAP_OFFSETS = [
    (first, second, third) for first in range(3) for second in range(3) for third in range(3)
]


def extended(block, sides, width):
    for axis, dim in sides:
        count = lax.axis_size(axis)
        forward = [(i, i + 1) for i in range(count - 1)]
        backward = [(target, source) for source, target in forward]
        low = lax.ppermute(
            lax.slice_in_dim(block, block.shape[dim] - width, None, axis=dim), axis, forward
        )
        high = lax.ppermute(lax.slice_in_dim(block, 0, width, axis=dim), axis, backward)
        block = jnp.concatenate([low, block, high], axis=dim)
    return block


def on_device(volume, kernel, bias, cotangent):
    local_volume = volume[0]
    channels_in, slab_depth, height, breadth = local_volume.shape
    outer = extended(local_volume, (("space", 1),), 1)
    padded = jnp.pad(outer, ((0, 0), (0, 0), (1, 1), (1, 1)))
    filters = kernel.shape[0]
    plane_cells = height * breadth // 4
    cells = 2 * height * breadth
    block_count = slab_depth // 2

    def compute_block(index, incoming):
        window = lax.dynamic_slice_in_dim(padded, index * 2, 4, 1)
        patches = jnp.concatenate(
            [
                window[:, sd : sd + 2, sh : sh + height, sw : sw + breadth]
                for sd, sh, sw in TAP_OFFSETS
            ],
            axis=0,
        ).reshape(27 * channels_in, cells)
        conv_out = jnp.dot(kernel, patches, preferred_element_type=jnp.float32) + bias[:, None]
        positive = conv_out > 0
        activated = jnp.where(positive, conv_out, 0.3 * conv_out).astype(jnp.bfloat16)
        pooled_block = activated.astype(jnp.float32).reshape(
            filters, 1, 2, height // 2, 2, breadth // 2, 2
        )
        pooled_block = (
            pooled_block.mean(axis=(2, 4, 6)).astype(jnp.bfloat16).reshape(filters, 1, plane_cells)
        )
        scaled = (
            incoming.astype(jnp.float32).reshape(filters, 1, 1, height // 2, 1, breadth // 2, 1)
            * 0.125
        )
        widened = jnp.broadcast_to(
            scaled, (filters, 1, 2, height // 2, 2, breadth // 2, 2)
        ).reshape(filters, cells)
        spread = (widened * jnp.where(positive, 1.0, 0.3)).astype(jnp.bfloat16)
        kernel_part = lax.dot_general(
            spread, patches, (((1,), (1,)), ((), ())), preferred_element_type=jnp.float32
        )
        bias_part = jnp.sum(spread.astype(jnp.float32), axis=1)
        return (pooled_block, kernel_part, bias_part)

    zero_kernel = jnp.zeros((filters, 27 * channels_in), jnp.float32)
    zero_bias = jnp.zeros((filters,), jnp.float32)
    returned = lax.all_to_all(cotangent[0], "space", split_axis=1, concat_axis=0, tiled=True)

    def advance(index, carry):
        pooled_buffer, kernel_sum, bias_sum = carry
        incoming = lax.dynamic_slice_in_dim(returned, index, 1, 1)
        pooled_block, kernel_part, bias_part = compute_block(index, incoming)
        pooled_buffer = lax.dynamic_update_slice_in_dim(pooled_buffer, pooled_block, index, 1)
        return (pooled_buffer, kernel_sum + kernel_part, bias_sum + bias_part)

    start_state = (
        jnp.zeros((filters, block_count, plane_cells), jnp.bfloat16),
        zero_kernel,
        zero_bias,
    )
    pooled_slab, kernel_sum, bias_sum = lax.fori_loop(0, block_count, advance, start_state)
    pooled_owned = lax.all_to_all(pooled_slab, "space", split_axis=0, concat_axis=1, tiled=True)
    kernel_grad, bias_grad = lax.psum((kernel_sum, bias_sum), ("space", "batch"))
    return (pooled_owned[None], kernel_grad, bias_grad)


def solution(mesh):
    placed = (P("batch", None, "space", None, None), P(), P(), P("batch", "space", None, None))
    return jax.shard_map(
        on_device,
        mesh=mesh,
        in_specs=placed,
        out_specs=(P("batch", "space", None, None), P(), P()),
        check_vma=False,
    )
```

profile of v0, /device:TPU:0, one launch (start us, length us, event | category | flops | bytes accessed | tf_op | source)
XLA Modules:
  0.0 169.3 jit_solution(3386673849513310016)
XLA Ops:
  0.7 1.8 %copy.44 = bf16[1,8,16,1024]{3,1,2,0:T(8,128)(2,1)} copy(bf16[1,8,16,1024]{3,2,1,0:T(8,128)(2,1)} %param.9) | data formatting | bytes 524288 | tf_op args[3]
  2.5 6.3 %all-to-all-start = ((bf16[8,16,1024]{2,0,1:T(8,128)(2,1)}), bf16[8,16,1024]{2,0,1:T(8,128)(2,1)S(1)}, u32[]{:S(2)}, u32[]{:S(2)}) async-start(bf16[8,16,1024]{2,0,1:T(8,128)(2,1)} %bitcast.25), calls=%async_computation | async-start | bytes 524288 | tf_op jit(solution)/shard_map/all_to_all | solution.py:68
  8.8 0.8 fusion.13
  9.6 3.9 %collective-permute-start = (bf16[4,1,32,128]{3,2,1,0:T(8,128)(2,1)S(1)}, bf16[4,1,32,128]{3,2,1,0:T(8,128)(2,1)S(1)}, u32[]{:S(2)}, u32[]{:S(2)}) collective-permute-start(bf16[4,1,32,128]{3,2,1,0:T(8,128)(2,1)S(1)} %get-tuple-element.227), channel_id=1, source_target_pairs={{0,8},{8,16},{16,24},{1,9},{9,17},{17,25},{2,10},{10,18},{18,26},{... | collective-permute-start | bytes 98312 | tf_op jit(solution)/shard_map/ppermute | solution.py:16
  13.5 1.3 collective-permute-start.1
  14.8 0.2 collective-permute-done
  15.1 4.2 %collective-permute-done.1 = bf16[4,1,32,128]{3,2,1,0:T(8,128)(2,1)S(1)} collective-permute-done((bf16[4,1,32,128]{3,2,1,0:T(8,128)(2,1)S(1)}, bf16[4,1,32,128]{3,2,1,0:T(8,128)(2,1)S(1)}, u32[]{:S(2)}, u32[]{:S(2)}) %collective-permute-start.1) | collective-permute-done | bytes 32800 | tf_op jit(solution)/shard_map/ppermute | solution.py:19
  19.3 1.5 select_maximum_fusion
  20.9 100.9 %while.18 = (s32[]{:T(128)}, bf16[32,4,1024]{2,0,1:T(8,128)(2,1)}, f32[32,108]{1,0:T(8,128)S(1)}, f32[32]{0:T(128)S(1)}, bf16[4,10,34,130]{3,2,1,0:T(8,128)(2,1)...) while((s32[]{:T(128)}, bf16[32,4,1024]{2,0,1:T(8,128)(2,1)}, ...), condition=%wide.region_3.4_spmd.clone, body=%wide.region_0.3_spmd.clone.sunk | while | flops 116497192 | bytes 25267560 | solution.py:82
  23.8 1.5 copy.52
  25.5 4.0 %broadcast_in_dim.48 = f32[32,2,16,2,64,2]{0,5,4,3,2,1:T(2,128)} broadcast(f32[32,16,64]{0,2,1:T(8,128)S(1)} %bitcast.51), dimensions={0,2,4} | broadcast | bytes 1179648 | tf_op jit(solution)/shard_map/while/body/eval_jaxpr/broadcast_in_dim | solution.py:56
  29.5 3.6 %copy.51 = f32[32,8192]{1,0:T(8,128)} copy(f32[32,8192]{0,1:T(8,128)} %bitcast.47) | data formatting | bytes 2097152 | tf_op jit(solution)/shard_map/while/body/eval_jaxpr/broadcast_in_dim | solution.py:56
  33.1 2.8 %convert_reduce_fusion.2 = (f32[32]{0:T(128)S(1)}, bf16[32,8192]{1,0:T(8,128)(2,1)S(1)}, f32[32,8192]{1,0:T(8,128)}) fusion(f32[32,8192]{1,0:T(8,128)} %copy.51, f32[32]{0:T(128)S(1)} %get-tuple-element.322, bf16[108,8192]{1,0:T(8,128)(2,1)S(1)} %bitcast.48, bf16[32,108]{1,0:T(8,128)(2,1)S(1)} %get-tuple-element.321), kind=kOutput, calls=%fused_computation.8.clone.1 | convolution fusion | flops 59506656 | bytes 4398080 | tf_op jit(solution)/shard_map/while/body/eval_jaxpr/dot_general | solution.py:43
  35.9 0.7 convolution_add_fusion.3
  36.6 3.6 %copy.53 = f32[32,8192]{0,1:T(8,128)} copy(f32[32,8192]{1,0:T(8,128)} %get-tuple-element.281) | data formatting | bytes 2097152 | tf_op jit(solution)/shard_map/while/body/eval_jaxpr/reshape | solution.py:46
  40.2 4.8 %reduce_sum.30 = f32[32,16,64]{0,2,1:T(8,128)S(1)} reduce(f32[32,2,16,2,64,2]{0,5,4,3,2,1:T(2,128)} %bitcast.46, f32[]{:T(128)} %constant.66.clone.8..sunk), dimensions={1,3,5}, to_apply=%region_1.1 | reduce | flops 229376 | bytes 1179652 | tf_op jit(solution)/shard_map/while/body/eval_jaxpr/reduce_sum | solution.py:50
  45.1 0.2 copy.54
  45.5 0.6 constant_dynamic-update-slice_fusion.2
  49.0 1.5 copy.52
  50.8 4.0 %broadcast_in_dim.48 = f32[32,2,16,2,64,2]{0,5,4,3,2,1:T(2,128)} broadcast(f32[32,16,64]{0,2,1:T(8,128)S(1)} %bitcast.51), dimensions={0,2,4} | broadcast | bytes 1179648 | tf_op jit(solution)/shard_map/while/body/eval_jaxpr/broadcast_in_dim | solution.py:56
  54.7 3.6 %copy.51 = f32[32,8192]{1,0:T(8,128)} copy(f32[32,8192]{0,1:T(8,128)} %bitcast.47) | data formatting | bytes 2097152 | tf_op jit(solution)/shard_map/while/body/eval_jaxpr/broadcast_in_dim | solution.py:56
  58.3 2.8 %convert_reduce_fusion.2 = (f32[32]{0:T(128)S(1)}, bf16[32,8192]{1,0:T(8,128)(2,1)S(1)}, f32[32,8192]{1,0:T(8,128)}) fusion(f32[32,8192]{1,0:T(8,128)} %copy.51, f32[32]{0:T(128)S(1)} %get-tuple-element.322, bf16[108,8192]{1,0:T(8,128)(2,1)S(1)} %bitcast.48, bf16[32,108]{1,0:T(8,128)(2,1)S(1)} %get-tuple-element.321), kind=kOutput, calls=%fused_computation.8.clone.1 | convolution fusion | flops 59506656 | bytes 4398080 | tf_op jit(solution)/shard_map/while/body/eval_jaxpr/dot_general | solution.py:43
  61.1 0.7 convolution_add_fusion.3
  61.9 3.6 %copy.53 = f32[32,8192]{0,1:T(8,128)} copy(f32[32,8192]{1,0:T(8,128)} %get-tuple-element.281) | data formatting | bytes 2097152 | tf_op jit(solution)/shard_map/while/body/eval_jaxpr/reshape | solution.py:46
  65.5 4.8 %reduce_sum.30 = f32[32,16,64]{0,2,1:T(8,128)S(1)} reduce(f32[32,2,16,2,64,2]{0,5,4,3,2,1:T(2,128)} %bitcast.46, f32[]{:T(128)} %constant.66.clone.8..sunk), dimensions={1,3,5}, to_apply=%region_1.1 | reduce | flops 229376 | bytes 1179652 | tf_op jit(solution)/shard_map/while/body/eval_jaxpr/reduce_sum | solution.py:50
  70.3 0.2 copy.54
  70.7 0.6 constant_dynamic-update-slice_fusion.2
  74.2 1.5 copy.52
  76.0 4.0 %broadcast_in_dim.48 = f32[32,2,16,2,64,2]{0,5,4,3,2,1:T(2,128)} broadcast(f32[32,16,64]{0,2,1:T(8,128)S(1)} %bitcast.51), dimensions={0,2,4} | broadcast | bytes 1179648 | tf_op jit(solution)/shard_map/while/body/eval_jaxpr/broadcast_in_dim | solution.py:56
  80.0 3.6 %copy.51 = f32[32,8192]{1,0:T(8,128)} copy(f32[32,8192]{0,1:T(8,128)} %bitcast.47) | data formatting | bytes 2097152 | tf_op jit(solution)/shard_map/while/body/eval_jaxpr/broadcast_in_dim | solution.py:56
  83.6 2.8 %convert_reduce_fusion.2 = (f32[32]{0:T(128)S(1)}, bf16[32,8192]{1,0:T(8,128)(2,1)S(1)}, f32[32,8192]{1,0:T(8,128)}) fusion(f32[32,8192]{1,0:T(8,128)} %copy.51, f32[32]{0:T(128)S(1)} %get-tuple-element.322, bf16[108,8192]{1,0:T(8,128)(2,1)S(1)} %bitcast.48, bf16[32,108]{1,0:T(8,128)(2,1)S(1)} %get-tuple-element.321), kind=kOutput, calls=%fused_computation.8.clone.1 | convolution fusion | flops 59506656 | bytes 4398080 | tf_op jit(solution)/shard_map/while/body/eval_jaxpr/dot_general | solution.py:43
  86.3 0.7 convolution_add_fusion.3
  87.1 3.6 %copy.53 = f32[32,8192]{0,1:T(8,128)} copy(f32[32,8192]{1,0:T(8,128)} %get-tuple-element.281) | data formatting | bytes 2097152 | tf_op jit(solution)/shard_map/while/body/eval_jaxpr/reshape | solution.py:46
  90.7 4.8 %reduce_sum.30 = f32[32,16,64]{0,2,1:T(8,128)S(1)} reduce(f32[32,2,16,2,64,2]{0,5,4,3,2,1:T(2,128)} %bitcast.46, f32[]{:T(128)} %constant.66.clone.8..sunk), dimensions={1,3,5}, to_apply=%region_1.1 | reduce | flops 229376 | bytes 1179652 | tf_op jit(solution)/shard_map/while/body/eval_jaxpr/reduce_sum | solution.py:50
  95.5 0.2 copy.54
  95.9 0.6 constant_dynamic-update-slice_fusion.2
  99.4 1.5 copy.52
  101.2 4.0 %broadcast_in_dim.48 = f32[32,2,16,2,64,2]{0,5,4,3,2,1:T(2,128)} broadcast(f32[32,16,64]{0,2,1:T(8,128)S(1)} %bitcast.51), dimensions={0,2,4} | broadcast | bytes 1179648 | tf_op jit(solution)/shard_map/while/body/eval_jaxpr/broadcast_in_dim | solution.py:56
  105.2 3.6 %copy.51 = f32[32,8192]{1,0:T(8,128)} copy(f32[32,8192]{0,1:T(8,128)} %bitcast.47) | data formatting | bytes 2097152 | tf_op jit(solution)/shard_map/while/body/eval_jaxpr/broadcast_in_dim | solution.py:56
  108.8 2.8 %convert_reduce_fusion.2 = (f32[32]{0:T(128)S(1)}, bf16[32,8192]{1,0:T(8,128)(2,1)S(1)}, f32[32,8192]{1,0:T(8,128)}) fusion(f32[32,8192]{1,0:T(8,128)} %copy.51, f32[32]{0:T(128)S(1)} %get-tuple-element.322, bf16[108,8192]{1,0:T(8,128)(2,1)S(1)} %bitcast.48, bf16[32,108]{1,0:T(8,128)(2,1)S(1)} %get-tuple-element.321), kind=kOutput, calls=%fused_computation.8.clone.1 | convolution fusion | flops 59506656 | bytes 4398080 | tf_op jit(solution)/shard_map/while/body/eval_jaxpr/dot_general | solution.py:43
  111.6 0.7 convolution_add_fusion.3
  112.3 3.6 %copy.53 = f32[32,8192]{0,1:T(8,128)} copy(f32[32,8192]{1,0:T(8,128)} %get-tuple-element.281) | data formatting | bytes 2097152 | tf_op jit(solution)/shard_map/while/body/eval_jaxpr/reshape | solution.py:46
  115.9 4.8 %reduce_sum.30 = f32[32,16,64]{0,2,1:T(8,128)S(1)} reduce(f32[32,2,16,2,64,2]{0,5,4,3,2,1:T(2,128)} %bitcast.46, f32[]{:T(128)} %constant.66.clone.8..sunk), dimensions={1,3,5}, to_apply=%region_1.1 | reduce | flops 229376 | bytes 1179652 | tf_op jit(solution)/shard_map/while/body/eval_jaxpr/reduce_sum | solution.py:50
  121.2 0.6 constant_dynamic-update-slice_fusion.2
  121.8 1.8 %copy.37 = bf16[32,4,1024]{2,1,0:T(4,128)(2,1)} copy(bf16[32,4,1024]{2,0,1:T(8,128)(2,1)} %get-tuple-element.144) | data formatting | bytes 524288 | tf_op jit(solution)/shard_map/while | solution.py:82
  123.7 3.6 %all-to-all-start.1 = ((bf16[32,4,1024]{2,1,0:T(4,128)(2,1)}), bf16[32,4,1024]{2,1,0:T(4,128)(2,1)S(1)}, u32[]{:S(2)}, u32[]{:S(2)}) async-start(bf16[32,4,1024]{2,1,0:T(4,128)(2,1)} %copy.37), calls=%async_computation.1 | async-start | bytes 524288 | tf_op jit(solution)/shard_map/all_to_all | solution.py:83
  127.3 41.1 %all-reduce.1 = (f32[32,108]{1,0:T(8,128)}, f32[32]{0:T(128)}) all-reduce(f32[32,108]{1,0:T(8,128)S(1)} %get-tuple-element.145, f32[32]{0:T(128)S(1)} %get-tuple-element.146), channel_id=1, replica_groups=mesh['space'=4,'batch'=8] {'space','batch'}, use_global_device_ids=true, to_apply=%region_4.5 | all-reduce | flops 3488 | bytes 27904 | tf_op jit(solution)/shard_map/psum | solution.py:84
  168.5 0.8 broadcast_in_dim.41
  (148 shorter events, 13.1 us)
Async XLA Ops:
  0.6 20.2 %copy-start = (bf16[32,108]{1,0:T(8,128)(2,1)S(1)}, bf16[32,108]{1,0:T(8,128)(2,1)}, u32[]{:S(2)}) copy-start(bf16[32,108]{1,0:T(8,128)(2,1)} %param.7) | copy-start | bytes 20740
  0.6 20.2 %copy-start.1 = (f32[32]{0:T(128)S(1)}, f32[32]{0:T(128)}, u32[]{:S(2)}) copy-start(f32[32]{0:T(128)} %param.8) | copy-start | bytes 388
  2.5 18.4 %all-to-all-start = ((bf16[8,16,1024]{2,0,1:T(8,128)(2,1)}), bf16[8,16,1024]{2,0,1:T(8,128)(2,1)S(1)}, u32[]{:S(2)}, u32[]{:S(2)}) async-start(bf16[8,16,1024]{2,0,1:T(8,128)(2,1)} %bitcast.25), calls=%async_computation | async-start | bytes 524288 | tf_op jit(solution)/shard_map/all_to_all | solution.py:68
  9.6 5.5 %collective-permute-start = (bf16[4,1,32,128]{3,2,1,0:T(8,128)(2,1)S(1)}, bf16[4,1,32,128]{3,2,1,0:T(8,128)(2,1)S(1)}, u32[]{:S(2)}, u32[]{:S(2)}) collective-permute-start(bf16[4,1,32,128]{3,2,1,0:T(8,128)(2,1)S(1)} %get-tuple-element.227), channel_id=1, source_target_pairs={{0,8},{8,16},{16,24},{1,9},{9,17},{17,25},{2,10},{10,18},{18,26},{... | collective-permute-start | bytes 98312 | tf_op jit(solution)/shard_map/ppermute | solution.py:16
  13.5 5.8 %collective-permute-start.1 = (bf16[4,1,32,128]{3,2,1,0:T(8,128)(2,1)S(1)}, bf16[4,1,32,128]{3,2,1,0:T(8,128)(2,1)S(1)}, u32[]{:S(2)}, u32[]{:S(2)}) collective-permute-start(bf16[4,1,32,128]{3,2,1,0:T(8,128)(2,1)S(1)} %get-tuple-element.228), channel_id=1, source_target_pairs={{8,0},{16,8},{24,16},{9,1},{17,9},{25,17},{10,2},{18,10},{26,18},{... | collective-permute-start | bytes 98312 | tf_op jit(solution)/shard_map/ppermute | solution.py:19
  123.7 44.7 %all-to-all-start.1 = ((bf16[32,4,1024]{2,1,0:T(4,128)(2,1)}), bf16[32,4,1024]{2,1,0:T(4,128)(2,1)S(1)}, u32[]{:S(2)}, u32[]{:S(2)}) async-start(bf16[32,4,1024]{2,1,0:T(4,128)(2,1)} %copy.37), calls=%async_computation.1 | async-start | bytes 524288 | tf_op jit(solution)/shard_map/all_to_all | solution.py:83
where the time goes:
time: 170 us; the launch traced here: 169 us
  local copies, waits for them, and re-layouts  71.9 us (42%)
  blocking collectives  41.1 us (24%)
  other arithmetic  21.2 us (12%)
  starting transfers between devices  15.2 us (9%)
  matrix products  14 us (8%)
  waiting for transfers between devices  4.48 us (3%)
    psum x1, blocking collectives, on_device(): lax.psum((kernel_sum, bias_sum), ('space', 'batch'))  41.1 us
    broadcast_in_dim x8, local copies, waits for them, and re-layouts, compute_block(): jnp.broadcast_to(scaled, (filters, 1, 2, height // 2, 2, breadth // 2, 2))  30.3 us
    reduce_sum x4, other arithmetic, compute_block(): pooled_block.mean(axis=(2, 4, 6)).astype(jnp.bfloat16)  19.4 us
    while x112, local copies, waits for them, and re-layouts  16.6 us
    reshape x4, local copies, waits for them, and re-layouts, compute_block(): activated.astype(jnp.float32)  14.4 us
    dot_general x4, matrix products, compute_block(): jnp.dot(kernel, patches, preferred_element_type=jnp.float32) + bias[:, None]  11.1 us
    all_to_all x1, starting transfers between devices, on_device(): lax.all_to_all(cotangent[0], 'space', split_axis=1, concat_axis=0, tiled=...  6.32 us
    ppermute x1, waiting for transfers between devices, extended(): lax.ppermute(lax.slice_in_dim(block, 0, width, axis=dim), axis, backward)  4.23 us
  transfers between devices with their start and end apart: 4, of which 2 were waited for; matrix products, arithmetic and copies ran while one was open for 1% of the time, Pallas kernels for 0%

commit v1 on v0

v1 whole, which is shorter than its diff:
```python
import functools

import jax
import jax.numpy as jnp
from jax import lax
from jax.experimental import pallas as pl
from jax.experimental.pallas import tpu as pltpu
from jax.sharding import PartitionSpec as P

MESH = pl.DeviceIdType.MESH
F32, BF16, I32 = jnp.float32, jnp.bfloat16, jnp.int32


def iota(shape, dim):
    return lax.broadcasted_iota(I32, shape, dim)


def onehot(rows, columns, source, value=1.0):
    return jnp.where(
        iota((rows, columns), 1) == source(iota((rows, columns), 0)), value, 0.0
    ).astype(BF16)


def fused_kernel(
    dims, vol_ref, ker_ref, bias_ref, cot_ref, pooled_ref, kg_ref, bg_ref,
    halo_lo, halo_hi, planes, patches, signs, cot_send, cot_recv, pool_flat,
    pool_send, pool_recv, part_recv, row_recv,
    halo_ssem, halo_rsem, cot_ssem, cot_rsem, pool_ssem, pool_rsem,
    part_ssem, part_rsem, row_ssem, row_rsem,
):
    spaces, batches, cin, slab, height, breadth, filters, group, pdepth, plane = dims
    local = slab // 2
    rows = local * filters
    block_rows = local * group
    groups = slab // 2 + 1
    kdim = 64 * cin
    taps = 27 * cin
    z = lax.axis_index("space")
    b = lax.axis_index("batch")

    barrier = pltpu.get_barrier_semaphore()
    for k in range(1, spaces):
        pl.semaphore_signal(
            barrier, inc=1, device_id={"space": lax.rem(z + k, spaces)}, device_id_type=MESH
        )
    for k in range(1, batches):
        pl.semaphore_signal(
            barrier, inc=1, device_id={"batch": lax.rem(b + k, batches)}, device_id_type=MESH
        )

    def by_slab(r):
        s = r // block_rows
        p = (r // group) % local
        return (r % group) * pdepth + s * local + p

    cotangent = cot_ref[0].reshape(rows, plane)
    cot_send[...] = (
        jnp.dot(onehot(rows, rows, by_slab), cotangent, preferred_element_type=F32)
        .astype(BF16)
        .reshape(spaces, block_rows, plane)
    )
    pl.semaphore_wait(barrier, spaces + batches - 2)

    up = pltpu.make_async_remote_copy(
        src_ref=vol_ref.at[0, :, slab - 1], dst_ref=halo_lo,
        send_sem=halo_ssem.at[0], recv_sem=halo_rsem.at[0],
        device_id={"space": lax.rem(z + 1, spaces)}, device_id_type=MESH,
    )
    down = pltpu.make_async_remote_copy(
        src_ref=vol_ref.at[0, :, 0], dst_ref=halo_hi,
        send_sem=halo_ssem.at[1], recv_sem=halo_rsem.at[1],
        device_id={"space": lax.rem(z + spaces - 1, spaces)}, device_id_type=MESH,
    )

    @pl.when(z < spaces - 1)
    def _():
        up.start()

    @pl.when(z > 0)
    def _():
        down.start()

    def exchange(send, recv, ssem, rsem):
        copies = []
        for k in range(1, spaces):
            to = lax.rem(z + k, spaces)
            copies.append(
                pltpu.make_async_remote_copy(
                    src_ref=send.at[to], dst_ref=recv.at[z],
                    send_sem=ssem.at[k], recv_sem=rsem.at[k],
                    device_id={"space": to}, device_id_type=MESH,
                )
            )
        return copies

    cot_copies = exchange(cot_send, cot_recv, cot_ssem, cot_rsem)
    for copy in cot_copies:
        copy.start()
    cot_recv[z] = cot_send[z]

    def spread_tap(lane):
        bb, ee, aa = lane // (16 * cin), (lane // (4 * cin)) % 4, (lane // cin) % 4
        inside = (aa < 3) & (bb < 3) & (ee < 3)
        return jnp.where(inside, (aa * 9 + bb * 3 + ee) * cin + lane % cin, -1)

    place = jnp.where(
        iota((taps, kdim), 0) == spread_tap(iota((taps, kdim), 1)), 1.0, 0.0
    ).astype(BF16)
    base = jnp.dot(ker_ref[...], place, preferred_element_type=F32)
    parities = [(pd, ph, pw) for pd in range(2) for ph in range(2) for pw in range(2)]
    shifts = [ph * 16 * cin + pw * 4 * cin + pd * cin for pd, ph, pw in parities]
    weights = jnp.concatenate(
        [base if s == 0 else pltpu.roll(base, s, 1) for s in shifts], axis=0
    ).astype(BF16)
    bias = jnp.sum(
        jnp.where(iota((filters, filters), 0) == iota((filters, filters), 1), bias_ref[...], 0.0),
        axis=1, keepdims=True,
    )

    pair_rows = 2 * cin * height
    turn = onehot(
        pair_rows, pair_rows,
        lambda r: (r % cin) * (2 * height) + ((r // cin) % 2) * height + r // (2 * cin),
    )

    def pair(first, second):
        pieces = []
        for c in range(cin):
            pieces += [first(c), second(c)]
        return jnp.concatenate(pieces, axis=0)

    def own(d):
        return lambda c: vol_ref[0, c, d]

    def turned(pairs):
        out = jnp.dot(turn, jnp.concatenate(pairs, axis=1), preferred_element_type=F32)
        return [
            out[:, i * breadth : (i + 1) * breadth].reshape(height, 2 * cin, breadth)
            for i in range(len(pairs))
        ]

    inner = turned([pair(own(2 * g - 1), own(2 * g)) for g in range(1, groups - 1)])

    @pl.when(z > 0)
    def _():
        up.wait_recv()

    @pl.when(z == 0)
    def _():
        halo_lo[...] = jnp.zeros_like(halo_lo)

    @pl.when(z < spaces - 1)
    def _():
        down.wait_recv()

    @pl.when(z == spaces - 1)
    def _():
        halo_hi[...] = jnp.zeros_like(halo_hi)

    outer = turned([pair(lambda c: halo_lo[c], own(0)), pair(own(slab - 1), lambda c: halo_hi[c])])
    all_groups = [outer[0], *inner, outer[1]]
    stack = planes.shape[1]
    if stack > groups * 2 * cin:
        all_groups.append(jnp.zeros((height, stack - groups * 2 * cin, breadth), F32))
    planes[0] = jnp.zeros((stack, breadth), BF16)
    planes[height + 1] = jnp.zeros((stack, breadth), BF16)
    planes[1 : height + 1] = jnp.concatenate(all_groups, axis=1).astype(BF16)

    half = breadth // 2

    def split_lane(lane):
        we, side, j = lane // breadth, (lane // half) % 2, lane % half
        w = 2 * j + we - 1
        return jnp.where((w >= 0) & (w < breadth), side * breadth + w, -1)

    select = jnp.where(
        iota((2 * breadth, 4 * breadth), 0) == split_lane(iota((2 * breadth, 4 * breadth), 1)),
        1.0, 0.0,
    ).astype(BF16)
    tiles = height // 4
    krows = 4 * cin
    for wh in range(4):
        left = jnp.concatenate(
            [
                jnp.concatenate([planes[4 * t + wh], planes[4 * t + wh + 2]], axis=1)
                for t in range(tiles)
            ],
            axis=0,
        )
        picked = jnp.dot(left, select, preferred_element_type=F32)
        for t in range(tiles):
            for we in range(4):
                for p in range(local):
                    start = t * stack + p * 2 * cin
                    patches[
                        p, (wh * 4 + we) * krows : (wh * 4 + we + 1) * krows,
                        t * breadth : (t + 1) * breadth,
                    ] = picked[start : start + krows, we * breadth : (we + 1) * breadth].astype(BF16)

    step = 256
    chunks = plane // step
    for p in range(local):
        for n in range(chunks):
            lanes = slice(n * step, (n + 1) * step)
            conv = jnp.dot(weights, patches[p, :, lanes], preferred_element_type=F32)
            total = None
            for i in range(8):
                part = conv[i * filters : (i + 1) * filters] + bias
                signs[p, i * filters : (i + 1) * filters, lanes] = part.astype(BF16)
                active = jnp.maximum(part, 0.3 * part)
                total = active if total is None else total + active
            pool_flat[p * filters : (p + 1) * filters, lanes] = (total * 0.125).astype(BF16)

    def by_owner(r):
        s = r // block_rows
        p = (r // group) % local
        return p * filters + s * group + r % group

    pool_send[...] = (
        jnp.dot(onehot(rows, rows, by_owner), pool_flat[...], preferred_element_type=F32)
        .astype(BF16)
        .reshape(spaces, block_rows, plane)
    )
    pool_copies = exchange(pool_send, pool_recv, pool_ssem, pool_rsem)
    for copy in pool_copies:
        copy.start()
    pool_recv[z] = pool_send[z]

    for copy in cot_copies:
        copy.wait_recv()

    def by_depth(r):
        p, o = r // filters, r % filters
        return (o // group) * block_rows + p * group + o % group

    u = jnp.dot(
        onehot(rows, rows, by_depth, 0.125), cot_recv[...].reshape(rows, plane),
        preferred_element_type=F32,
    )
    low = (0.3 * u).astype(BF16).astype(F32)
    grad = jnp.zeros((8 * filters, kdim), F32)
    bias_sum = jnp.zeros((filters, step), F32)
    for p in range(local):
        for n in range(chunks):
            lanes = slice(n * step, (n + 1) * step)
            up_value = u[p * filters : (p + 1) * filters, lanes]
            low_value = low[p * filters : (p + 1) * filters, lanes]
            spread = []
            for i in range(8):
                sign = signs[p, i * filters : (i + 1) * filters, lanes].astype(F32)
                one = jnp.where(sign > 0, up_value, low_value)
                bias_sum = bias_sum + one
                spread.append(one.astype(BF16))
            grad = grad + lax.dot_general(
                jnp.concatenate(spread, axis=0), patches[p, :, lanes],
                (((1,), (1,)), ((), ())), preferred_element_type=F32,
            )

    folded = None
    for i, s in enumerate(shifts):
        part = grad[i * filters : (i + 1) * filters]
        part = part if s == 0 else pltpu.roll(part, kdim - s, 1)
        folded = part if folded is None else folded + part
    width = part_recv.shape[2]
    collect = jnp.where(
        iota((kdim, width), 1) == spread_tap(iota((kdim, width), 0)), 1.0, 0.0
    )
    compact = jnp.dot(
        folded, collect, preferred_element_type=F32, precision=lax.Precision.HIGHEST
    )
    bias_column = jnp.sum(bias_sum, axis=1, keepdims=True)
    part_recv[b] = compact + jnp.where(iota((filters, width), 1) == taps, bias_column, 0.0)

    part_copies = []
    for k in range(1, batches):
        part_copies.append(
            pltpu.make_async_remote_copy(
                src_ref=part_recv.at[b], dst_ref=part_recv.at[b],
                send_sem=part_ssem.at[k], recv_sem=part_rsem.at[k],
                device_id={"batch": lax.rem(b + k, batches)}, device_id_type=MESH,
            )
        )
    for copy in part_copies:
        copy.start()
    for copy in part_copies:
        copy.wait_recv()
    total = part_recv[0]
    for k in range(1, batches):
        total = total + part_recv[k]
    row_recv[z] = total
    row_copies = []
    for k in range(1, spaces):
        row_copies.append(
            pltpu.make_async_remote_copy(
                src_ref=row_recv.at[z], dst_ref=row_recv.at[z],
                send_sem=row_ssem.at[k], recv_sem=row_rsem.at[k],
                device_id={"space": lax.rem(z + k, spaces)}, device_id_type=MESH,
            )
        )
    for copy in row_copies:
        copy.start()

    for copy in pool_copies:
        copy.wait_recv()

    def by_channel(r):
        ol, s, p = r // pdepth, (r // local) % spaces, r % local
        return s * block_rows + p * group + ol

    pooled_ref[0] = (
        jnp.dot(
            onehot(rows, rows, by_channel), pool_recv[...].reshape(rows, plane),
            preferred_element_type=F32,
        )
        .astype(BF16)
        .reshape(group, pdepth, plane)
    )

    for copy in row_copies:
        copy.wait_recv()
    total = row_recv[0]
    for k in range(1, spaces):
        total = total + row_recv[k]
    kg_ref[...] = total[:, :taps]
    bg_ref[...] = jnp.sum(
        jnp.where(
            iota((filters, filters), 0) == iota((filters, filters), 1),
            total[:, taps : taps + 1], 0.0,
        ),
        axis=0, keepdims=True,
    )

    @pl.when(z < spaces - 1)
    def _():
        up.wait_send()

    @pl.when(z > 0)
    def _():
        down.wait_send()

    for copy in cot_copies + pool_copies + part_copies + row_copies:
        copy.wait_send()


def solution(mesh):
    spaces, batches = mesh.shape["space"], mesh.shape["batch"]

    def on_device(volume, kernel, bias, cotangent):
        _, cin, slab, height, breadth = volume.shape
        filters = kernel.shape[0]
        _, group, pdepth, plane = cotangent.shape
        taps = kernel.shape[1]
        width = -(-(taps + 1) // 128) * 128
        local = slab // 2
        block = (spaces, local * group, plane)
        stack = -(-((slab + 2) * cin) // 16) * 16
        dma = pltpu.SemaphoreType.DMA
        vmem = pl.BlockSpec(memory_space=pltpu.VMEM)
        pooled, kernel_grad, bias_grad = pl.pallas_call(
            functools.partial(
                fused_kernel,
                (spaces, batches, cin, slab, height, breadth, filters, group, pdepth, plane),
            ),
            out_shape=(
                jax.ShapeDtypeStruct(cotangent.shape, BF16),
                jax.ShapeDtypeStruct(kernel.shape, F32),
                jax.ShapeDtypeStruct((1, filters), F32),
            ),
            in_specs=[vmem] * 4,
            out_specs=(vmem, vmem, vmem),
            scratch_shapes=[
                pltpu.VMEM((cin, height, breadth), BF16),
                pltpu.VMEM((cin, height, breadth), BF16),
                pltpu.VMEM((height + 2, stack, breadth), BF16),
                pltpu.VMEM((local, 64 * cin, plane), BF16),
                pltpu.VMEM((local, 8 * filters, plane), BF16),
                pltpu.VMEM(block, BF16),
                pltpu.VMEM(block, BF16),
                pltpu.VMEM((local * filters, plane), BF16),
                pltpu.VMEM(block, BF16),
                pltpu.VMEM(block, BF16),
                pltpu.VMEM((batches, filters, width), F32),
                pltpu.VMEM((spaces, filters, width), F32),
                dma((2,)), dma((2,)),
                dma((spaces,)), dma((spaces,)),
                dma((spaces,)), dma((spaces,)),
                dma((batches,)), dma((batches,)),
                dma((spaces,)), dma((spaces,)),
            ],
            compiler_params=pltpu.CompilerParams(
                collective_id=0, has_side_effects=True, vmem_limit_bytes=40 * 2**20
            ),
        )(volume, kernel, bias.reshape(1, filters), cotangent)
        return pooled, kernel_grad, bias_grad.reshape(filters)

    placed = (P("batch", None, "space", None, None), P(), P(), P("batch", "space", None, None))
    return jax.shard_map(
        on_device,
        mesh=mesh,
        in_specs=placed,
        out_specs=(P("batch", "space", None, None), P(), P()),
        check_vma=False,
    )
```

time: 170 us -> 30.8 us (0.18)
  local copies, waits for them, and re-layouts: 71.9 us -> 5.06 us
  blocking collectives: 41.1 us -> 0 us
  Pallas kernels: 0 us -> 24.8 us
  other arithmetic: 21.2 us -> 0 us
  starting transfers between devices: 15.2 us -> 0 us
  matrix products: 14 us -> 0 us
  waiting for transfers between devices: 4.48 us -> 0 us
    psum x1 -> x0, blocking collectives: 41.1 us -> none  [on_device(): lax.psum((kernel_sum, bias_sum), ('space', 'batch'))]
    broadcast_in_dim x9 -> x0, local copies, waits for them, and re-layouts: 31.1 us -> none  [the longest x8 30.3 us: compute_block(): jnp.broadcast_to(scaled, (filters, 1, 2, height // 2, 2, breadth // 2, 2))]
    pallas_call x0 -> x1, Pallas kernels: none -> 24.8 us  [on_device(): pl.pallas_call(functools.partial(fused_kernel, (spaces, batches, cin, sla...]
    reduce_sum x4 -> x0, other arithmetic: 19.4 us -> none  [compute_block(): pooled_block.mean(axis=(2, 4, 6)).astype(jnp.bfloat16)]
    while x113 -> x0, local copies, waits for them, and re-layouts: 18.5 us -> none
    reshape x4 -> x0, local copies, waits for them, and re-layouts: 14.4 us -> none  [compute_block(): activated.astype(jnp.float32)]
    dot_general x8 -> x0, matrix products: 14 us -> none  [the longest x4 11.1 us: compute_block(): jnp.dot(kernel, patches, preferred_element_type=jnp.float32) + bias[:, None]]
    all_to_all x2 -> x0, starting transfers between devices: 9.95 us -> none  [the longest x1 6.32 us: on_device(): lax.all_to_all(cotangent[0], 'space', split_axis=1, concat_axis=0, tiled=...]
  transfers between devices with their start and end apart: 4 -> 0, of which waited for: 2 -> 0; matrix products, arithmetic and copies ran while one was open for 1% -> 0% of each run, Pallas kernels for 0% -> 0%
where the time goes in v1:
time: 30.8 us; the launch traced here: 30.6 us
  Pallas kernels  24.8 us (81%)
  local copies, waits for them, and re-layouts  5.06 us (16%)
  between operations  0.65 us (2%)
    pallas_call x1, Pallas kernels, on_device(): pl.pallas_call(functools.partial(fused_kernel, (spaces, batches, cin, sla...  24.8 us
    unnamed x11, local copies, waits for them, and re-layouts  5.06 us

profile of v1, /device:TPU:0, one launch (start us, length us, event | category | flops | bytes accessed | tf_op | source)
XLA Modules:
  0.0 30.6 jit_solution(10399829762639461099)
XLA Ops:
  0.6 0.0 copy-start.3
  0.6 0.6 %copy-done.3 = f32[32]{0:T(128)S(1)} copy-done((f32[32]{0:T(128)S(1)}, f32[32]{0:T(128)}, u32[]{:S(2)}) %copy-start.3) | copy-done | bytes 152
  1.3 0.0 copy-start
  1.3 0.9 %copy-done = bf16[1,4,8,32,128]{4,3,2,1,0:T(8,128)(2,1)S(1)} copy-done((bf16[1,4,8,32,128]{4,3,2,1,0:T(8,128)(2,1)S(1)}, bf16[1,4,8,32,128]{4,3,2,1,0:T(8,128)(2,1)}, u32[]{:S(2)}) %copy-start) | copy-done | bytes 262168
  2.2 0.0 copy-start.1
  2.2 0.9 %copy-done.1 = bf16[1,8,16,1024]{3,2,1,0:T(8,128)(2,1)S(1)} copy-done((bf16[1,8,16,1024]{3,2,1,0:T(8,128)(2,1)S(1)}, bf16[1,8,16,1024]{3,2,1,0:T(8,128)(2,1)}, u32[]{:S(2)}) %copy-start.1) | copy-done | bytes 262168
  3.2 0.0 copy-start.2
  3.2 0.7 %copy-done.2 = bf16[32,108]{1,0:T(8,128)(2,1)S(1)} copy-done((bf16[32,108]{1,0:T(8,128)(2,1)S(1)}, bf16[32,108]{1,0:T(8,128)(2,1)}, u32[]{:S(2)}) %copy-start.2) | copy-done | bytes 6936
  3.9 24.8 %shard_map.67 = (bf16[1,8,16,1024]{3,2,1,0:T(8,128)(2,1)S(1)}, f32[32,108]{1,0:T(8,128)S(1)}, f32[1,32]{1,0:T(1,128)S(1)}) custom-call(bf16[1,4,8,32,128]{4,3,2,1,0:T(8,128)(2,1)S(1)} %copy-done, bf16[32,108]{1,0:T(8,128)(2,1)S(1)} %copy-done.2, f32[1,32]{1,0:T(1,128)S(1)} %bitcast.2, bf16[1,8,16,1024]{3,2,1,0:T(8,128)(2,1)S(1)} %copy-done.1), custom_call_target="tpu_custom_call" | custom-call | tf_op jit(solution)/shard_map/pallas_call | solution.py:359
  28.7 0.7 %copy.10 = bf16[1,8,16,1024]{3,2,1,0:T(8,128)(2,1)} copy(bf16[1,8,16,1024]{3,2,1,0:T(8,128)(2,1)S(1)} %get-tuple-element.12) | data formatting | bytes 524288
  29.4 0.6 %copy.11 = f32[32,108]{1,0:T(8,128)} copy(f32[32,108]{1,0:T(8,128)S(1)} %get-tuple-element.13) | data formatting | bytes 27648
  30.0 0.5 %copy.12 = f32[32]{0:T(128)} copy(f32[32]{0:T(128)S(1)} %bitcast.3) | data formatting | bytes 256
Async XLA Ops:
  0.6 0.7 %copy-start.3 = (f32[32]{0:T(128)S(1)}, f32[32]{0:T(128)}, u32[]{:S(2)}) copy-start(f32[32]{0:T(128)} %param.6) | copy-start | bytes 388
  1.3 0.9 %copy-start = (bf16[1,4,8,32,128]{4,3,2,1,0:T(8,128)(2,1)S(1)}, bf16[1,4,8,32,128]{4,3,2,1,0:T(8,128)(2,1)}, u32[]{:S(2)}) copy-start(bf16[1,4,8,32,128]{4,3,2,1,0:T(8,128)(2,1)} %vol_ref.1) | copy-start | bytes 786436
  2.2 0.9 %copy-start.1 = (bf16[1,8,16,1024]{3,2,1,0:T(8,128)(2,1)S(1)}, bf16[1,8,16,1024]{3,2,1,0:T(8,128)(2,1)}, u32[]{:S(2)}) copy-start(bf16[1,8,16,1024]{3,2,1,0:T(8,128)(2,1)} %cot_ref.1) | copy-start | bytes 786436
  3.2 0.7 %copy-start.2 = (bf16[32,108]{1,0:T(8,128)(2,1)S(1)}, bf16[32,108]{1,0:T(8,128)(2,1)}, u32[]{:S(2)}) copy-start(bf16[32,108]{1,0:T(8,128)(2,1)} %ker_ref.1) | copy-start | bytes 20740

commit v2 on v1

--- a/solution.py
+++ b/solution.py
@@ -8,6 +8,7 @@
 from jax.sharding import PartitionSpec as P
 
 MESH = pl.DeviceIdType.MESH
+LIMIT = 63 * 2**20
 F32, BF16, I32 = jnp.float32, jnp.bfloat16, jnp.int32
 
 
@@ -22,9 +23,9 @@
 
 
 def fused_kernel(
-    dims, vol_ref, ker_ref, bias_ref, cot_ref, pooled_ref, kg_ref, bg_ref,
-    halo_lo, halo_hi, planes, patches, signs, cot_send, cot_recv, pool_flat,
-    pool_send, pool_recv, part_recv, row_recv,
+    dims, vol_hbm, ker_hbm, bias_hbm, cot_hbm, pooled_out, kg_out, bg_out,
+    vol_ref, ker_ref, bias_ref, cot_ref, in_sem, halo_lo, halo_hi, planes, planes_in, patches, signs, cot_send, cot_recv, pool_flat,
+    pool_send, pool_recv, part_recv, row_recv, pooled_ref, kg_ref, bg_ref, out_sem,
     halo_ssem, halo_rsem, cot_ssem, cot_rsem, pool_ssem, pool_rsem,
     part_ssem, part_rsem, row_ssem, row_rsem,
 ):
@@ -38,6 +39,15 @@
     z = lax.axis_index("space")
     b = lax.axis_index("batch")
 
+    loads = [
+        pltpu.make_async_copy(source, target, in_sem.at[i])
+        for i, (source, target) in enumerate(
+            [(cot_hbm, cot_ref), (vol_hbm, vol_ref), (ker_hbm, ker_ref), (bias_hbm, bias_ref)]
+        )
+    ]
+    for load in loads:
+        load.start()
+
     barrier = pltpu.get_barrier_semaphore()
     for k in range(1, spaces):
         pl.semaphore_signal(
@@ -53,6 +63,7 @@
         p = (r // group) % local
         return (r % group) * pdepth + s * local + p
 
+    loads[0].wait()
     cotangent = cot_ref[0].reshape(rows, plane)
     cot_send[...] = (
         jnp.dot(onehot(rows, rows, by_slab), cotangent, preferred_element_type=F32)
@@ -62,12 +73,12 @@
     pl.semaphore_wait(barrier, spaces + batches - 2)
 
     up = pltpu.make_async_remote_copy(
-        src_ref=vol_ref.at[0, :, slab - 1], dst_ref=halo_lo,
+        src_ref=vol_hbm.at[0, :, slab - 1], dst_ref=halo_lo,
         send_sem=halo_ssem.at[0], recv_sem=halo_rsem.at[0],
         device_id={"space": lax.rem(z + 1, spaces)}, device_id_type=MESH,
     )
     down = pltpu.make_async_remote_copy(
-        src_ref=vol_ref.at[0, :, 0], dst_ref=halo_hi,
+        src_ref=vol_hbm.at[0, :, 0], dst_ref=halo_hi,
         send_sem=halo_ssem.at[1], recv_sem=halo_rsem.at[1],
         device_id={"space": lax.rem(z + spaces - 1, spaces)}, device_id_type=MESH,
     )
@@ -103,6 +114,8 @@
         inside = (aa < 3) & (bb < 3) & (ee < 3)
         return jnp.where(inside, (aa * 9 + bb * 3 + ee) * cin + lane % cin, -1)
 
+    for load in loads[1:]:
+        load.wait()
     place = jnp.where(
         iota((taps, kdim), 0) == spread_tap(iota((taps, kdim), 1)), 1.0, 0.0
     ).astype(BF16)
@@ -141,31 +154,6 @@
 
     inner = turned([pair(own(2 * g - 1), own(2 * g)) for g in range(1, groups - 1)])
 
-    @pl.when(z > 0)
-    def _():
-        up.wait_recv()
-
-    @pl.when(z == 0)
-    def _():
-        halo_lo[...] = jnp.zeros_like(halo_lo)
-
-    @pl.when(z < spaces - 1)
-    def _():
-        down.wait_recv()
-
-    @pl.when(z == spaces - 1)
-    def _():
-        halo_hi[...] = jnp.zeros_like(halo_hi)
-
-    outer = turned([pair(lambda c: halo_lo[c], own(0)), pair(own(slab - 1), lambda c: halo_hi[c])])
-    all_groups = [outer[0], *inner, outer[1]]
-    stack = planes.shape[1]
-    if stack > groups * 2 * cin:
-        all_groups.append(jnp.zeros((height, stack - groups * 2 * cin, breadth), F32))
-    planes[0] = jnp.zeros((stack, breadth), BF16)
-    planes[height + 1] = jnp.zeros((stack, breadth), BF16)
-    planes[1 : height + 1] = jnp.concatenate(all_groups, axis=1).astype(BF16)
-
     half = breadth // 2
 
     def split_lane(lane):
@@ -179,37 +167,69 @@
     ).astype(BF16)
     tiles = height // 4
     krows = 4 * cin
-    for wh in range(4):
-        left = jnp.concatenate(
-            [
-                jnp.concatenate([planes[4 * t + wh], planes[4 * t + wh + 2]], axis=1)
-                for t in range(tiles)
-            ],
-            axis=0,
-        )
-        picked = jnp.dot(left, select, preferred_element_type=F32)
-        for t in range(tiles):
-            for we in range(4):
-                for p in range(local):
-                    start = t * stack + p * 2 * cin
-                    patches[
-                        p, (wh * 4 + we) * krows : (wh * 4 + we + 1) * krows,
-                        t * breadth : (t + 1) * breadth,
-                    ] = picked[start : start + krows, we * breadth : (we + 1) * breadth].astype(BF16)
-
     step = 256
     chunks = plane // step
-    for p in range(local):
-        for n in range(chunks):
-            lanes = slice(n * step, (n + 1) * step)
-            conv = jnp.dot(weights, patches[p, :, lanes], preferred_element_type=F32)
-            total = None
-            for i in range(8):
-                part = conv[i * filters : (i + 1) * filters] + bias
-                signs[p, i * filters : (i + 1) * filters, lanes] = part.astype(BF16)
-                active = jnp.maximum(part, 0.3 * part)
-                total = active if total is None else total + active
-            pool_flat[p * filters : (p + 1) * filters, lanes] = (total * 0.125).astype(BF16)
+
+    def forward(held, members, depths):
+        stack = held.shape[1]
+        members = list(members)
+        if stack > len(members) * 2 * cin:
+            members.append(jnp.zeros((height, stack - len(members) * 2 * cin, breadth), F32))
+        held[0] = jnp.zeros((stack, breadth), BF16)
+        held[height + 1] = jnp.zeros((stack, breadth), BF16)
+        held[1 : height + 1] = jnp.concatenate(members, axis=1).astype(BF16)
+        for wh in range(4):
+            left = jnp.concatenate(
+                [
+                    jnp.concatenate([held[4 * t + wh], held[4 * t + wh + 2]], axis=1)
+                    for t in range(tiles)
+                ],
+                axis=0,
+            )
+            picked = jnp.dot(left, select, preferred_element_type=F32)
+            for t in range(tiles):
+                for we in range(4):
+                    for p, first in depths:
+                        start = t * stack + first * 2 * cin
+                        patches[
+                            p, (wh * 4 + we) * krows : (wh * 4 + we + 1) * krows,
+                            t * breadth : (t + 1) * breadth,
+                        ] = picked[
+                            start : start + krows, we * breadth : (we + 1) * breadth
+                        ].astype(BF16)
+        for p, _ in depths:
+            for n in range(chunks):
+                lanes = slice(n * step, (n + 1) * step)
+                conv = jnp.dot(weights, patches[p, :, lanes], preferred_element_type=F32)
+                total = None
+                for i in range(8):
+                    part = conv[i * filters : (i + 1) * filters] + bias
+                    signs[p, i * filters : (i + 1) * filters, lanes] = part.astype(BF16)
+                    active = jnp.maximum(part, 0.3 * part)
+                    total = active if total is None else total + active
+                pool_flat[p * filters : (p + 1) * filters, lanes] = (total * 0.125).astype(BF16)
+
+    if local > 2:
+        forward(planes_in, inner, [(p, p - 1) for p in range(1, local - 1)])
+
+    @pl.when(z > 0)
+    def _():
+        up.wait_recv()
+
+    @pl.when(z == 0)
+    def _():
+        halo_lo[...] = jnp.zeros_like(halo_lo)
+
+    @pl.when(z < spaces - 1)
+    def _():
+        down.wait_recv()
+
+    @pl.when(z == spaces - 1)
+    def _():
+        halo_hi[...] = jnp.zeros_like(halo_hi)
+
+    outer = turned([pair(lambda c: halo_lo[c], own(0)), pair(own(slab - 1), lambda c: halo_hi[c])])
+    forward(planes, [outer[0], inner[0], inner[-1], outer[1]], [(0, 0), (local - 1, 2)])
 
     def by_owner(r):
         s = r // block_rows
@@ -300,6 +320,12 @@
     for copy in row_copies:
         copy.start()
 
+    stores = [
+        pltpu.make_async_copy(source, target, out_sem.at[i])
+        for i, (source, target) in enumerate(
+            [(kg_ref, kg_out), (bg_ref, bg_out), (pooled_ref, pooled_out)]
+        )
+    ]
     for copy in pool_copies:
         copy.wait_recv()
 
@@ -315,6 +341,7 @@
         .astype(BF16)
         .reshape(group, pdepth, plane)
     )
+    stores[2].start()
 
     for copy in row_copies:
         copy.wait_recv()
@@ -329,6 +356,8 @@
         ),
         axis=0, keepdims=True,
     )
+    stores[0].start()
+    stores[1].start()
 
     @pl.when(z < spaces - 1)
     def _():
@@ -340,6 +369,19 @@
 
     for copy in cot_copies + pool_copies + part_copies + row_copies:
         copy.wait_send()
+    for store in stores:
+        store.wait()
+
+
+def finish_kernel(*refs):
+    count = (len(refs) - 1) // 2
+    copies = [
+        pltpu.make_async_copy(refs[i], refs[count + i], refs[-1].at[i]) for i in range(count)
+    ]
+    for copy in copies:
+        copy.start()
+    for copy in copies:
+        copy.wait()
 
 
 def solution(mesh):
@@ -353,24 +395,31 @@
         width = -(-(taps + 1) // 128) * 128
         local = slab // 2
         block = (spaces, local * group, plane)
-        stack = -(-((slab + 2) * cin) // 16) * 16
+        stack = -(-(max(local - 1, 1) * 2 * cin) // 16) * 16
         dma = pltpu.SemaphoreType.DMA
-        vmem = pl.BlockSpec(memory_space=pltpu.VMEM)
-        pooled, kernel_grad, bias_grad = pl.pallas_call(
+        hbm = pl.BlockSpec(memory_space=pltpu.HBM)
+        shapes = (
+            jax.ShapeDtypeStruct(cotangent.shape, BF16),
+            jax.ShapeDtypeStruct(kernel.shape, F32),
+            jax.ShapeDtypeStruct((1, filters), F32),
+        )
+        results = pl.pallas_call(
             functools.partial(
                 fused_kernel,
                 (spaces, batches, cin, slab, height, breadth, filters, group, pdepth, plane),
             ),
-            out_shape=(
-                jax.ShapeDtypeStruct(cotangent.shape, BF16),
-                jax.ShapeDtypeStruct(kernel.shape, F32),
-                jax.ShapeDtypeStruct((1, filters), F32),
-            ),
-            in_specs=[vmem] * 4,
-            out_specs=(vmem, vmem, vmem),
+            out_shape=shapes,
+            in_specs=[hbm] * 4,
+            out_specs=(hbm,) * 3,
             scratch_shapes=[
+                pltpu.VMEM(volume.shape, BF16),
+                pltpu.VMEM(kernel.shape, BF16),
+                pltpu.VMEM((1, filters), F32),
+                pltpu.VMEM(cotangent.shape, BF16),
+                dma((4,)),
                 pltpu.VMEM((cin, height, breadth), BF16),
                 pltpu.VMEM((cin, height, breadth), BF16),
+                pltpu.VMEM((height + 2, 8 * cin, breadth), BF16),
                 pltpu.VMEM((height + 2, stack, breadth), BF16),
                 pltpu.VMEM((local, 64 * cin, plane), BF16),
                 pltpu.VMEM((local, 8 * filters, plane), BF16),
@@ -381,6 +430,10 @@
                 pltpu.VMEM(block, BF16),
                 pltpu.VMEM((batches, filters, width), F32),
                 pltpu.VMEM((spaces, filters, width), F32),
+                pltpu.VMEM(cotangent.shape, BF16),
+                pltpu.VMEM(kernel.shape, F32),
+                pltpu.VMEM((1, filters), F32),
+                dma((3,)),
                 dma((2,)), dma((2,)),
                 dma((spaces,)), dma((spaces,)),
                 dma((spaces,)), dma((spaces,)),
@@ -388,9 +441,17 @@
                 dma((spaces,)), dma((spaces,)),
             ],
             compiler_params=pltpu.CompilerParams(
-                collective_id=0, has_side_effects=True, vmem_limit_bytes=40 * 2**20
+                collective_id=0, has_side_effects=True, vmem_limit_bytes=LIMIT
             ),
         )(volume, kernel, bias.reshape(1, filters), cotangent)
+        pooled, kernel_grad, bias_grad = pl.pallas_call(
+            finish_kernel,
+            out_shape=shapes,
+            in_specs=[hbm] * 3,
+            out_specs=(hbm,) * 3,
+            scratch_shapes=[dma((3,))],
+            compiler_params=pltpu.CompilerParams(vmem_limit_bytes=LIMIT),
+        )(*results)
         return pooled, kernel_grad, bias_grad.reshape(filters)
 
     placed = (P("batch", None, "space", None, None), P(), P(), P("batch", "space", None, None))

time: 30.8 us -> 36.2 us (1.18)
  Pallas kernels: 24.8 us -> 35.4 us
  local copies, waits for them, and re-layouts: 5.06 us -> 0 us
    pallas_call x0 -> x1, Pallas kernels: none -> 9.58 us  [on_device(): pl.pallas_call(finish_kernel, out_shape=shapes, in_specs=[hbm] * 3, out_s...]
    unnamed x11 -> x0, local copies, waits for them, and re-layouts: 5.06 us -> none
    pallas_call x1, Pallas kernels: 24.8 us -> 25.8 us  [on_device(): pl.pallas_call(functools.partial(fused_kernel, (spaces, batches, cin, sla...]
where the time goes in v2:
time: 36.2 us; the launch traced here: 36 us
  Pallas kernels  35.4 us (98%)
  between operations  0.64 us (2%)
    pallas_call x1, Pallas kernels, on_device(): pl.pallas_call(functools.partial(fused_kernel, (spaces, batches, cin, sla...  25.8 us
    pallas_call x1, Pallas kernels, on_device(): pl.pallas_call(finish_kernel, out_shape=shapes, in_specs=[hbm] * 3, out_s...  9.58 us

profile of v2, /device:TPU:0, one launch (start us, length us, event | category | flops | bytes accessed | tf_op | source)
XLA Modules:
  0.0 36.0 jit_solution(11335928732112480552)
XLA Ops:
  0.6 25.8 %shard_map.67 = (bf16[1,8,16,1024]{3,2,1,0:T(8,128)(2,1)}, f32[32,108]{1,0:T(8,128)}, f32[1,32]{1,0:T(1,128)}) custom-call(bf16[1,4,8,32,128]{4,3,2,1,0:T(8,128)(2,1)} %vol_hbm.1, bf16[32,108]{1,0:T(8,128)(2,1)} %ker_hbm.1, f32[1,32]{1,0:T(1,128)} %bitcast.2, bf16[1,8,16,1024]{3,2,1,0:T(8,128)(2,1)} %cot_hbm.1), custom_call_target="tpu_custom_call" | custom-call | tf_op jit(solution)/shard_map/pallas_call | solution.py:406
  26.4 9.6 %shard_map.68 = (bf16[1,8,16,1024]{3,2,1,0:T(8,128)(2,1)}, f32[32,108]{1,0:T(8,128)}, f32[1,32]{1,0:T(1,128)}) custom-call(bf16[1,8,16,1024]{3,2,1,0:T(8,128)(2,1)} %get-tuple-element.9.refs_0_, f32[32,108]{1,0:T(8,128)} %get-tuple-element.10.refs_1_, f32[1,32]{1,0:T(1,128)} %get-tuple-element.11.refs_2_), custom_call_target="tpu_custom_call" | custom-call | tf_op jit(solution)/shard_map/pallas_call | solution.py:447
